TPU v7x, 32 devices: a whole 2x2x4 slice. The times are simulated.
32 devices in a mesh: row: 4 (over y, core), col: 8 (over z, x).
Axes of the slice: x: 2, y: 2, z: 4, core: 2. Of those that a mesh axis runs over, the one named last changes fastest.
Arguments:
- b_three: bfloat16 [64, 384, 1536], P(('row', 'col')), may hold values from -0.47851562 to 0.47851562
- e_occ: float32 [64], replicated, may hold values from -1.5 to -0.3
- e_vir: float32 [384], replicated, may hold values from 0.2 to 3
- c_occ: bfloat16 [768, 64], replicated, may hold values from -0.75 to 0.75
- pair_list: int32 [32, 8, 2], P(('row', 'col')), may hold values from 0 to 63, as said below
- pair_live: int32 [32, 8], P(('row', 'col')), may hold values from 0 to 1, as said below
Outputs:
- gamma_ao: bfloat16 [384, 1536, 768], P('row', 'col')
Inputs may be any that keep to these rules, and one draw needn't show every extreme that they name: pair_list[w, p, 0] is one of the orbitals 2 w to 2 w + 1; pair_list[w, p, 1] is one of the orbitals 2 q to 2 q + 1 with q = (w // 8) * 8 + p. `pair_live`: every worker lists between 1 and 8 pairs; some worker lists all 8.
All inputs are finite; a program needn't handle non-finite values.
Results may differ from a plain program's by a relative error of at most 0.0053.
Values may be sent and summed in bfloat16 or wider, within the bound.
A program may use at most 128 MiB of HBM per device.

v0:
```python
import jax
import jax.numpy as jnp
from jax import lax
from jax.sharding import PartitionSpec as P


def local(b_three, e_occ, e_vir, c_occ, pair_list, pair_live):
    own_count = b_three.shape[0]
    virt_count = b_three.shape[1]
    aux_count = b_three.shape[2]
    peer_count = lax.axis_size("col")
    row_count = lax.axis_size("row")

    def pair_step(gamma, peer, right_slab):
        first_orb = pair_list[0, peer, 0]
        second_orb = pair_list[0, peer, 1]
        listed_flag = pair_live[0, peer]
        own_slot = first_orb % own_count
        left_slab = lax.dynamic_index_in_dim(b_three, own_slot, 0, keepdims=False)
        integrals = lax.dot_general(
            left_slab, right_slab, (((1,), (1,)), ((), ())), preferred_element_type=jnp.float32
        )
        denominator = e_occ[first_orb] + e_occ[second_orb] - e_vir[:, None] - e_vir[None, :]
        amplitude = integrals / denominator
        weighted = (2.0 * amplitude - amplitude.T).astype(jnp.bfloat16)
        addition = jnp.dot(weighted, right_slab, preferred_element_type=jnp.float32)
        current = lax.dynamic_index_in_dim(gamma, own_slot, 0, keepdims=False)
        return lax.dynamic_update_index_in_dim(
            gamma, current + listed_flag.astype(jnp.float32) * addition, own_slot, 0
        )

    gamma = jnp.zeros(b_three.shape, jnp.float32)
    wanted = (pair_list[0, :, 1] % own_count).reshape(peer_count, 1)
    asked = lax.all_to_all(wanted, "col", split_axis=0, concat_axis=0, tiled=True)
    outgoing = jnp.take(b_three, asked[:, 0], axis=0)
    arrived = lax.all_to_all(outgoing, "col", split_axis=0, concat_axis=0, tiled=True)

    def visit_arrived(position, gamma):
        right_slab = lax.dynamic_index_in_dim(arrived, position, 0, keepdims=False)
        return pair_step(gamma, position, right_slab)

    gamma = lax.fori_loop(0, peer_count, visit_arrived, gamma)
    gamma_mo = gamma.astype(jnp.bfloat16)
    virt_local = virt_count // row_count
    aux_local = aux_count // peer_count
    total_orbs = c_occ.shape[1]
    blocks = gamma_mo.reshape(own_count, row_count, virt_local, peer_count, aux_local)
    blocks = jnp.transpose(blocks, (1, 3, 0, 2, 4)).reshape(
        row_count * peer_count, own_count, virt_local * aux_local
    )
    regrouped = lax.all_to_all(blocks, ("row", "col"), split_axis=0, concat_axis=0, tiled=True)
    moved = regrouped.reshape(total_orbs, virt_local * aux_local)
    result = lax.dot_general(
        moved, c_occ, (((0,), (1,)), ((), ())), preferred_element_type=jnp.float32
    ).astype(jnp.bfloat16)
    return result.reshape(virt_local, aux_local, c_occ.shape[0])


def solution(mesh):
    return jax.shard_map(
        local,
        mesh=mesh,
        in_specs=(
            P(("row", "col"), None, None),
            P(),
            P(),
            P(),
            P(("row", "col"), None, None),
            P(("row", "col"), None),
        ),
        out_specs=P("row", "col", None),
        check_vma=False,
    )
```

profile of v0, /device:TPU:0, one launch (start us, length us, event | category | flops | bytes accessed | tf_op | source)
XLA Modules:
  0.0 494.2 jit_solution(243237323112716079)
XLA Ops:
  0.8 13.5 %all_to_all.22 = s32[8,1,1]{2,1,0:T(1,128)S(1)} all-to-all(s32[8,1,1]{2,1,0:T(1,128)S(1)} %copy.18), channel_id=1, replica_groups=mesh['row'=4,'col'=8] {'col'}, dimensions={0} | all-to-all | bytes 64 | tf_op jit(solution)/shard_map/all_to_all | solution.py:34
  14.6 6.8 %gather_fusion = bf16[8,384,1536]{2,1,0:T(8,128)(2,1)} fusion(bf16[2,384,1536]{2,1,0:T(8,128)(2,1)} %param.8, s32[1024]{0:T(1024)S(1)} %pad_clamp_fusion), kind=kCustom, calls=%fused_computation | custom fusion | bytes 18874400 | tf_op jit(solution)/shard_map/jit(_take)/gather | solution.py:35
  21.4 8.4 %broadcast_select_fusion = bf16[8,384,1536]{2,1,0:T(8,128)(2,1)} fusion(bf16[8,384,1536]{2,1,0:T(8,128)(2,1)} %gather_fusion, pred[8]{0:T(512)(128)(4,1)S(1)} %compare_and_fusion), kind=kLoop, calls=%fused_computation.29 | loop fusion | flops 4718592 | bytes 18874376 | tf_op jit(solution)/shard_map/jit(_take)/select_n | solution.py:35
  29.8 5.0 %all-to-all-start.1 = ((bf16[8,384,1536]{2,1,0:T(8,128)(2,1)}), bf16[8,384,1536]{2,1,0:T(8,128)(2,1)}, u32[]{:S(2)}, u32[]{:S(2)}) async-start(bf16[8,384,1536]{2,1,0:T(8,128)(2,1)} %broadcast_select_fusion), calls=%async_computation.1 | async-start | bytes 18874368 | tf_op jit(solution)/shard_map/all_to_all | solution.py:36
  34.9 204.3 %all-to-all-done.1 = bf16[8,384,1536]{2,1,0:T(8,128)(2,1)} async-done(((bf16[8,384,1536]{2,1,0:T(8,128)(2,1)}), bf16[8,384,1536]{2,1,0:T(8,128)(2,1)}, u32[]{:S(2)}, u32[]{:S(2)}) %all-to-all-start.1) | async-done | bytes 9437216 | tf_op jit(solution)/shard_map/all_to_all | solution.py:36
  239.2 2.8 broadcast_in_dim.30
  242.0 158.3 %while.15 = (s32[]{:T(128)}, f32[2,384,1536]{2,1,0:T(8,128)}, s32[1,8,2]{1,2,0:T(2,128)S(1)}, s32[1,8]{1,0:T(1,128)S(1)}, bf16[2,384,1536]{2,1,0:T(8,128)(2,1)S(...) while((s32[]{:T(128)}, f32[2,384,1536]{2,1,0:T(8,128)}, ...), condition=%wide.region_1.2_spmd, body=%wide.region_0.1_spmd.sunk | while | flops 908181888 | bytes 53686224 | solution.py:42
  250.3 2.1 fusion.40
  253.5 2.0 constant_dynamic-slice_fusion.7
  255.4 1.1 copy-done.1
  256.5 3.1 fusion.42
  259.6 2.2 copy-done.2
  270.1 2.1 fusion.40
  273.3 2.0 constant_dynamic-slice_fusion.7
  276.3 3.1 fusion.42
  279.4 2.2 copy-done.2
  289.9 2.1 fusion.40
  293.0 2.0 constant_dynamic-slice_fusion.7
  296.1 3.1 fusion.42
  299.2 2.2 copy-done.2
  309.7 2.1 fusion.40
  312.8 2.0 constant_dynamic-slice_fusion.7
  315.9 3.1 fusion.42
  319.0 2.2 copy-done.2
  329.5 2.1 fusion.40
  332.6 2.0 constant_dynamic-slice_fusion.7
  335.7 3.1 fusion.42
  338.8 2.2 copy-done.2
  349.3 2.1 fusion.40
  352.4 2.0 constant_dynamic-slice_fusion.7
  355.5 3.1 fusion.42
  358.6 2.2 copy-done.2
  369.1 2.1 fusion.40
  372.2 2.0 constant_dynamic-slice_fusion.7
  375.2 3.1 fusion.42
  378.4 2.2 copy-done.2
  388.8 2.1 fusion.40
  392.0 2.0 constant_dynamic-slice_fusion.7
  395.0 3.1 fusion.42
  398.2 2.2 copy-done.2
  400.3 4.0 convert_element_type.29
  404.4 4.7 reshape.110
  409.1 2.5 copy.22
  411.6 5.1 %reshape.111 = bf16[32,2,18432]{2,0,1:T(8,128)(2,1)S(1)} reshape(bf16[4,8,2,96,192]{4,3,1,0,2:T(8,128)(2,1)} %bitcast.61) | data formatting | bytes 4718592 | tf_op jit(solution)/shard_map/reshape | solution.py:48
  416.7 2.4 copy.20
  419.2 59.3 %all_to_all.23 = bf16[32,2,18432]{2,1,0:T(2,128)(2,1)} all-to-all(bf16[32,2,18432]{2,1,0:T(2,128)(2,1)S(1)} %copy.20), channel_id=1, replica_groups=mesh['row'=4,'col'=8] {'row','col'}, dimensions={0} | all-to-all | bytes 4718592 | tf_op jit(solution)/shard_map/all_to_all | solution.py:51
  478.5 2.9 reshape.112
  481.4 12.8 %convolution_convert_fusion = bf16[18432,768]{1,0:T(8,128)(2,1)} fusion(bf16[64,18432]{1,0:T(8,128)(2,1)S(1)} %reshape.112, bf16[768,64]{0,1:T(8,128)(2,1)S(1)} %copy-done), kind=kOutput, calls=%fused_computation.28 | convolution fusion | flops 1826095104 | bytes 30769152 | tf_op jit(solution)/shard_map/dot_general | solution.py:53
  (81 shorter events, 32.9 us)
Async XLA Ops:
  0.0 481.4 %copy-start = (bf16[768,64]{0,1:T(8,128)(2,1)S(1)}, bf16[768,64]{0,1:T(8,128)(2,1)}, u32[]{:S(2)}) copy-start(bf16[768,64]{0,1:T(8,128)(2,1)} %param.11) | copy-start | bytes 294916
  29.8 209.4 %all-to-all-start.1 = ((bf16[8,384,1536]{2,1,0:T(8,128)(2,1)}), bf16[8,384,1536]{2,1,0:T(8,128)(2,1)}, u32[]{:S(2)}, u32[]{:S(2)}) async-start(bf16[8,384,1536]{2,1,0:T(8,128)(2,1)} %broadcast_select_fusion), calls=%async_computation.1 | async-start | bytes 18874368 | tf_op jit(solution)/shard_map/all_to_all | solution.py:36
  34.8 207.2 %copy-start.3 = (bf16[2,384,1536]{2,1,0:T(8,128)(2,1)S(1)}, bf16[2,384,1536]{2,1,0:T(8,128)(2,1)}, u32[]{:S(2)}) copy-start(bf16[2,384,1536]{2,1,0:T(8,128)(2,1)} %param.8) | copy-start | bytes 7077892
  34.8 207.1 %copy-start.4 = (f32[64]{0:T(128)S(1)}, f32[64]{0:T(128)}, u32[]{:S(2)}) copy-start(f32[64]{0:T(128)} %param.9) | copy-start | bytes 772
  34.9 207.1 %copy-start.5 = (f32[384]{0:T(512)S(1)}, f32[384]{0:T(512)}, u32[]{:S(2)}) copy-start(f32[384]{0:T(512)} %param.10) | copy-start | bytes 4612
  34.9 207.1 %copy-start.6 = (s32[1,8,2]{1,2,0:T(2,128)S(1)}, s32[1,8,2]{1,2,0:T(2,128)}, u32[]{:S(2)}) copy-start(s32[1,8,2]{1,2,0:T(2,128)} %param.12) | copy-start | bytes 196
  34.9 207.1 %copy-start.7 = (s32[1,8]{1,0:T(1,128)S(1)}, s32[1,8]{1,0:T(1,128)}, u32[]{:S(2)}) copy-start(s32[1,8]{1,0:T(1,128)} %param.13) | copy-start | bytes 100
  253.5 3.0 copy-start.1
  259.6 2.2 copy-start.2
  273.3 3.0 copy-start.1
  279.4 2.2 copy-start.2
  293.0 3.0 copy-start.1
  299.2 2.2 copy-start.2
  312.8 3.0 copy-start.1
  319.0 2.2 copy-start.2
  332.6 3.0 copy-start.1
  338.8 2.2 copy-start.2
  352.4 3.0 copy-start.1
  358.6 2.2 copy-start.2
  372.2 3.0 copy-start.1
  378.4 2.2 copy-start.2
  392.0 3.0 copy-start.1
  398.1 2.2 copy-start.2
where the time goes:
time: 496 us; the launch traced here: 494 us
  waiting for transfers between devices  204 us (41%)
  local copies, waits for them, and re-layouts  88 us (18%)
  blocking collectives  72.8 us (15%)
  matrix products  54.2 us (11%)
  loops' own time  50.9 us (10%)
  other arithmetic  18.7 us (4%)
  starting transfers between devices  5.05 us (1%)
    all_to_all x1, waiting for transfers between devices, local(): lax.all_to_all(outgoing, 'col', split_axis=0, concat_axis=0, tiled=True)  204 us
    all_to_all x1, blocking collectives, local(): lax.all_to_all(blocks, ('row', 'col'), split_axis=0, concat_axis=0, tiled...  59.3 us
    another operation x1, loops' own time, local(): gamma = lax.fori_loop(0, peer_count, visit_arrived, gamma)  50.9 us
    while x32, local copies, waits for them, and re-layouts  26 us
    dot_general x8, matrix products, pair_step(): addition = jnp.dot(weighted, right_slab, preferred_element_type=jnp.float32)  24.9 us
    dot_general x8, matrix products, pair_step(): lax.dot_general(left_slab, right_slab, (((1,), (1,)), ((), ())), preferre...  16.5 us
    dynamic_slice x8, local copies, waits for them, and re-layouts, pair_step(): current = lax.dynamic_index_in_dim(gamma, own_slot, 0, keepdims=False)  15.7 us
    all_to_all x1, blocking collectives, local(): lax.all_to_all(wanted, 'col', split_axis=0, concat_axis=0, tiled=True)  13.5 us
  transfers between devices with their start and end apart: 1, of which 1 were waited for; matrix products, arithmetic and copies ran while one was open for 0% of the time, Pallas kernels for 0%

commit v1 on v0

v1 whole, which is shorter than its diff:
```python
import functools

import jax
import jax.numpy as jnp
from jax import lax
from jax.experimental import pallas as pl
from jax.experimental.pallas import tpu as pltpu
from jax.sharding import PartitionSpec as P

CHUNKS = 4


def grid_of(peer_count):
    nx = 1
    while (2 * nx) ** 2 <= peer_count:
        nx *= 2
    return peer_count // nx, nx


def exchange_kernel(
    nz, nx, want_ref, b_ref, right_ref, up_buf, dn_buf, stage,
    up_send, up_recv, dn_send, dn_recv, keep_sem, x_send, x_recv,
):
    own_count = b_ref.shape[0]
    rows = b_ref.shape[1] // CHUNKS
    col = lax.axis_index("col")
    z, x = col // nx, col % nx

    def at(zz, xx):
        return {"col": zz * nx + xx}

    def block(c):
        return pl.ds(pl.multiple_of(c * rows, rows), rows)

    barrier = pltpu.get_barrier_semaphore()

    @pl.when(z + 1 < nz)
    def _():
        pl.semaphore_signal(barrier, inc=1, device_id=at(z + 1, x))

    @pl.when(z > 0)
    def _():
        pl.semaphore_signal(barrier, inc=1, device_id=at(z - 1, x))

    for k in range(1, nx):
        pl.semaphore_signal(barrier, inc=1, device_id=at(z, (x + k) % nx))
    greeted = (nx - 1) + (z + 1 < nz).astype(jnp.int32) + (z > 0).astype(jnp.int32)
    pl.semaphore_wait(barrier, greeted)

    def up_copy(source, hop, c):
        return pltpu.make_async_remote_copy(
            src_ref=source, dst_ref=up_buf.at[hop, :, block(c), :],
            send_sem=up_send.at[hop, c], recv_sem=up_recv.at[hop, c],
            device_id=at(z + 1, x))

    def dn_copy(source, hop, c):
        return pltpu.make_async_remote_copy(
            src_ref=source, dst_ref=dn_buf.at[hop, :, block(c), :],
            send_sem=dn_send.at[hop, c], recv_sem=dn_recv.at[hop, c],
            device_id=at(z - 1, x))

    def keep_copy(zs, c):
        return pltpu.make_async_copy(
            stage.at[0, zs, block(c), :], right_ref.at[zs * nx + x, block(c), :],
            keep_sem.at[zs, c])

    def x_copy(k, zs, c):
        return pltpu.make_async_remote_copy(
            src_ref=stage.at[k, zs, block(c), :],
            dst_ref=right_ref.at[zs * nx + x, block(c), :],
            send_sem=x_send.at[k - 1, zs, c], recv_sem=x_recv.at[k - 1, zs, c],
            device_id=at(z, (x + k) % nx))

    def hand_on(load, zs, c):
        for k in list(range(1, nx)) + [0]:
            slot = want_ref[k, zs]
            picked = load(0)
            for orb in range(1, own_count):
                picked = jnp.where(slot == orb, load(orb), picked)
            stage[k, zs, block(c), :] = picked
            if k:
                x_copy(k, zs, c).start()
            else:
                keep_copy(zs, c).start()

    def begin(c, carry):
        @pl.when(z + 1 < nz)
        def _():
            up_copy(b_ref.at[:, block(c), :], 0, c).start()

        @pl.when(z > 0)
        def _():
            dn_copy(b_ref.at[:, block(c), :], 0, c).start()

        return carry

    lax.fori_loop(0, CHUNKS, begin, 0)

    def own(c, carry):
        hand_on(lambda orb: b_ref[orb, block(c), :], z, c)
        return carry

    lax.fori_loop(0, CHUNKS, own, 0)

    for hop in range(nz - 1):
        def arrive(c, carry, hop=hop):
            @pl.when(z - hop - 1 >= 0)
            def _():
                up_copy(up_buf.at[hop, :, block(c), :], hop, c).wait_recv()
                if hop + 1 < nz - 1:
                    @pl.when(z + 1 < nz)
                    def _():
                        up_copy(up_buf.at[hop, :, block(c), :], hop + 1, c).start()

            @pl.when(z + hop + 1 < nz)
            def _():
                dn_copy(dn_buf.at[hop, :, block(c), :], hop, c).wait_recv()
                if hop + 1 < nz - 1:
                    @pl.when(z > 0)
                    def _():
                        dn_copy(dn_buf.at[hop, :, block(c), :], hop + 1, c).start()

            @pl.when(z - hop - 1 >= 0)
            def _():
                hand_on(lambda orb: up_buf[hop, orb, block(c), :], z - hop - 1, c)

            @pl.when(z + hop + 1 < nz)
            def _():
                hand_on(lambda orb: dn_buf[hop, orb, block(c), :], z + hop + 1, c)

            return carry

        lax.fori_loop(0, CHUNKS, arrive, 0)

    def finish(c, carry):
        for zs in range(nz):
            keep_copy(zs, c).wait()
            for k in range(1, nx):
                x_copy(k, zs, c).wait()
        for hop in range(nz - 1):
            @pl.when((z + 1 < nz) & (z - hop >= 0))
            def _():
                up_copy(b_ref.at[:, block(c), :], hop, c).wait_send()

            @pl.when((z > 0) & (z + hop < nz))
            def _():
                dn_copy(b_ref.at[:, block(c), :], hop, c).wait_send()
        return carry

    lax.fori_loop(0, CHUNKS, finish, 0)


def exchange(b_three, want, nz, nx):
    own_count, virt, aux = b_three.shape
    dma = pltpu.SemaphoreType.DMA
    return pl.pallas_call(
        functools.partial(exchange_kernel, nz, nx),
        out_shape=jax.ShapeDtypeStruct((nz * nx, virt, aux), b_three.dtype),
        in_specs=[
            pl.BlockSpec(memory_space=pltpu.SMEM),
            pl.BlockSpec(memory_space=pltpu.VMEM),
        ],
        out_specs=pl.BlockSpec(memory_space=pl.ANY),
        scratch_shapes=[
            pltpu.VMEM((nz - 1, own_count, virt, aux), b_three.dtype),
            pltpu.VMEM((nz - 1, own_count, virt, aux), b_three.dtype),
            pltpu.VMEM((nx, nz, virt, aux), b_three.dtype),
            dma((nz - 1, CHUNKS)), dma((nz - 1, CHUNKS)),
            dma((nz - 1, CHUNKS)), dma((nz - 1, CHUNKS)),
            dma((nz, CHUNKS)),
            dma((nx - 1, nz, CHUNKS)), dma((nx - 1, nz, CHUNKS)),
        ],
        compiler_params=pltpu.CompilerParams(
            collective_id=0, has_side_effects=True, vmem_limit_bytes=56 << 20
        ),
    )(want, b_three)


def pairs_kernel(
    slot_ref, live_ref, esum_ref, b_ref, right_ref, evc_ref, evr_ref, out_ref, gamma
):
    p = pl.program_id(0)

    @pl.when(p == 0)
    def _():
        gamma[...] = jnp.zeros_like(gamma)

    @pl.when(live_ref[p] > 0)
    def _():
        slot = slot_ref[p]
        right = right_ref[0]
        integrals = lax.dot_general(
            b_ref[slot], right, (((1,), (1,)), ((), ())), preferred_element_type=jnp.float32
        )
        amplitude = integrals / (esum_ref[p] - evc_ref[...] - evr_ref[...])
        weighted = (2.0 * amplitude - amplitude.T).astype(jnp.bfloat16)
        gamma[slot] += jnp.dot(weighted, right, preferred_element_type=jnp.float32)

    @pl.when(p == pl.num_programs(0) - 1)
    def _():
        out_ref[...] = gamma[...].astype(out_ref.dtype)


def form_pairs(b_three, right, slot, live, esum, e_vir):
    own_count, virt, aux = b_three.shape
    peers = right.shape[0]
    whole = lambda p, *_: (0, 0, 0)
    flat = lambda p, *_: (0, 0)
    return pl.pallas_call(
        pairs_kernel,
        out_shape=jax.ShapeDtypeStruct(b_three.shape, jnp.bfloat16),
        grid_spec=pltpu.PrefetchScalarGridSpec(
            num_scalar_prefetch=3,
            grid=(peers,),
            in_specs=[
                pl.BlockSpec((own_count, virt, aux), whole),
                pl.BlockSpec((1, virt, aux), lambda p, *_: (p, 0, 0)),
                pl.BlockSpec((virt, 1), flat),
                pl.BlockSpec((1, virt), flat),
            ],
            out_specs=pl.BlockSpec((own_count, virt, aux), whole),
            scratch_shapes=[pltpu.VMEM((own_count, virt, aux), jnp.float32)],
        ),
        compiler_params=pltpu.CompilerParams(vmem_limit_bytes=56 << 20),
    )(slot, live, esum, b_three, right, e_vir[:, None], e_vir[None, :])


def local(b_three, e_occ, e_vir, c_occ, pair_list, pair_live):
    own_count, virt_count, aux_count = b_three.shape
    peer_count = lax.axis_size("col")
    row_count = lax.axis_size("row")
    nz, nx = grid_of(peer_count)

    first, second = pair_list[0, :, 0], pair_list[0, :, 1]
    x = lax.axis_index("col") % nx
    slots = (second % own_count).reshape(nz, nx)
    wants = [slots]
    for k in range(1, nx):
        back = [(z * nx + (c + k) % nx, z * nx + c) for z in range(nz) for c in range(nx)]
        wants.append(lax.ppermute(slots, "col", back))
    want = lax.dynamic_index_in_dim(jnp.stack(wants), x, 2, keepdims=False)
    right = exchange(b_three, want, nz, nx)
    gamma_mo = form_pairs(
        b_three, right, first % own_count, pair_live[0], e_occ[first] + e_occ[second], e_vir
    )

    virt_local = virt_count // row_count
    aux_local = aux_count // peer_count
    total_orbs = c_occ.shape[1]
    blocks = gamma_mo.reshape(own_count, row_count, virt_local, peer_count, aux_local)
    blocks = jnp.transpose(blocks, (1, 3, 0, 2, 4)).reshape(
        row_count * peer_count, own_count, virt_local * aux_local
    )
    regrouped = lax.all_to_all(blocks, ("row", "col"), split_axis=0, concat_axis=0, tiled=True)
    moved = regrouped.reshape(total_orbs, virt_local * aux_local)
    result = lax.dot_general(
        moved, c_occ, (((0,), (1,)), ((), ())), preferred_element_type=jnp.float32
    ).astype(jnp.bfloat16)
    return result.reshape(virt_local, aux_local, c_occ.shape[0])


def solution(mesh):
    return jax.shard_map(
        local,
        mesh=mesh,
        in_specs=(
            P(("row", "col"), None, None),
            P(),
            P(),
            P(),
            P(("row", "col"), None, None),
            P(("row", "col"), None),
        ),
        out_specs=P("row", "col", None),
        check_vma=False,
    )
```

time: 496 us -> 285 us (0.57)
  waiting for transfers between devices: 204 us -> 0.01 us
  Pallas kernels: 0 us -> 178 us
  local copies, waits for them, and re-layouts: 88 us -> 23.9 us
  loops' own time: 50.9 us -> 0 us
  matrix products: 54.2 us -> 12.8 us
  other arithmetic: 18.7 us -> 3.35 us
  blocking collectives: 72.8 us -> 62.9 us
    all_to_all x1 -> x0, waiting for transfers between devices: 204 us -> none  [local(): lax.all_to_all(outgoing, 'col', split_axis=0, concat_axis=0, tiled=True)]
    pallas_call x0 -> x2, Pallas kernels: none -> 178 us  [the longest x1 164 us: exchange(): pl.pallas_call(functools.partial(exchange_kernel, nz, nx), out_shape=jax....]
    another operation x1 -> x0, loops' own time: 50.9 us -> none  [local(): gamma = lax.fori_loop(0, peer_count, visit_arrived, gamma)]
    dot_general x16 -> x0, matrix products: 41.4 us -> none  [the longest x8 24.9 us: pair_step(): addition = jnp.dot(weighted, right_slab, preferred_element_type=jnp.float32)]
    dynamic_slice x24 -> x0, local copies, waits for them, and re-layouts: 26.2 us -> none  [the longest x8 15.7 us: pair_step(): current = lax.dynamic_index_in_dim(gamma, own_slot, 0, keepdims=False)]
    while x32 -> x0, local copies, waits for them, and re-layouts: 26 us -> none
    all_to_all x1 -> x0, blocking collectives: 13.5 us -> none  [local(): lax.all_to_all(wanted, 'col', split_axis=0, concat_axis=0, tiled=True)]
    convert_element_type x9 -> x0, other arithmetic: 9.33 us -> none  [the longest x8 5.31 us: pair_step(): listed_flag.astype(jnp.float32) * addition]
  transfers between devices with their start and end apart: 1 -> 1, of which waited for: 1 -> 0; matrix products, arithmetic and copies ran while one was open for 0% -> 3% of each run, Pallas kernels for 0% -> 0%
where the time goes in v1:
time: 285 us; the launch traced here: 284 us
  Pallas kernels  178 us (62%)
  blocking collectives  62.9 us (22%)
  local copies, waits for them, and re-layouts  23.9 us (8%)
  matrix products  12.8 us (4%)
  other arithmetic  3.35 us (1%)
  starting transfers between devices  2.99 us (1%)
    pallas_call x1, Pallas kernels, exchange(): pl.pallas_call(functools.partial(exchange_kernel, nz, nx), out_shape=jax....  164 us
    all_to_all x1, blocking collectives, local(): lax.all_to_all(blocks, ('row', 'col'), split_axis=0, concat_axis=0, tiled...  62.9 us
    pallas_call x1, Pallas kernels, form_pairs(): pl.pallas_call(pairs_kernel, out_shape=jax.ShapeDtypeStruct(b_three.shape...  14.1 us
    dot_general x1, matrix products, local(): lax.dot_general(moved, c_occ, (((0,), (1,)), ((), ())), preferred_element...  12.8 us
    reshape x2, local copies, waits for them, and re-layouts, local(): jnp.transpose(blocks, (1, 3, 0, 2, 4))  7.56 us
    reshape x2, local copies, waits for them, and re-layouts, local(): gamma_mo.reshape(own_count, row_count, virt_local, peer_count, aux_local)  7.22 us
  transfers between devices with their start and end apart: 1, of which 0 were waited for; matrix products, arithmetic and copies ran while one was open for 3% of the time, Pallas kernels for 0%

profile of v1, /device:TPU:0, one launch (start us, length us, event | category | flops | bytes accessed | tf_op | source)
XLA Modules:
  0.0 284.1 jit_solution(12126304986451548268)
XLA Ops:
  0.0 0.0 copy-start
  0.0 0.7 slice_reduce_fusion
  0.7 0.1 squeeze.24
  0.8 3.0 %collective-permute-start = (s32[4,2]{1,0:T(4,128)S(1)}, s32[4,2]{1,0:T(4,128)S(1)}, u32[]{:S(2)}, u32[]{:S(2)}) collective-permute-start(s32[4,2]{1,0:T(4,128)S(1)} %add_select_fusion), channel_id=1, source_target_pairs={{1,0},{0,1},{3,2},{2,3},{5,4},{4,5},{7,6},{6,7},{9,8},{8,9},{11,10... | collective-permute-start | bytes 104 | tf_op jit(solution)/shard_map/ppermute | solution.py:240
  3.8 1.2 and_select_fusion.slot_ref
  5.0 0.8 fusion.5
  5.8 1.3 broadcast_in_dim.9.evr_ref
  7.0 1.5 broadcast_in_dim.10.evc_ref
  8.5 0.1 squeeze.23
  8.6 1.3 gather_fusion.1
  9.9 1.3 gather_fusion
  11.2 0.6 add.54.esum_ref
  11.8 0.0 collective-permute-done
  11.8 0.8 fusion.want_ref
  12.6 164.0 %shard_map.64.right_ref = bf16[8,384,1536]{2,1,0:T(8,128)(2,1)} custom-call(s32[2,4]{1,0:T(2,128)} %fusion.want_ref, bf16[2,384,1536]{2,1,0:T(8,128)(2,1)} %b_ref.3), custom_call_target="tpu_custom_call" | custom-call | tf_op jit(solution)/shard_map/pallas_call | solution.py:156
  176.6 14.1 %shard_map.65 = bf16[2,384,1536]{2,1,0:T(8,128)(2,1)} custom-call(s32[8]{0:T(128)} %and_select_fusion.slot_ref, s32[8]{0:T(128)} %bitcast.26, f32[8]{0:T(128)} %add.54.esum_ref, bf16[2,384,1536]{2,1,0:T(8,128)(2,1)} %b_ref.3, bf16[8,384,1536]{2,1,0:T(8,128)(2,1)} %shard_map.64.right_ref, f32[384,1]{1,0:T(8,128)} %broadcast_in_dim.10.evc_ref, ...), custom_call_target="tpu_custom_call" | custom-call | tf_op jit(solution)/shard_map/pallas_call | solution.py:209
  190.7 4.7 %reshape.122 = bf16[2,4,96,8,192]{4,3,2,1,0:T(8,128)(2,1)S(1)} reshape(bf16[2,384,1536]{2,1,0:T(8,128)(2,1)} %shard_map.65) | data formatting | bytes 4718592 | tf_op jit(solution)/shard_map/reshape | solution.py:250
  195.4 2.5 copy.25
  197.9 5.1 %reshape.123 = bf16[32,2,18432]{2,0,1:T(8,128)(2,1)S(1)} reshape(bf16[4,8,2,96,192]{4,3,1,0,2:T(8,128)(2,1)} %bitcast.24) | data formatting | bytes 4718592 | tf_op jit(solution)/shard_map/reshape | solution.py:251
  203.1 2.4 copy.22
  205.5 62.9 %all_to_all.5 = bf16[32,2,18432]{2,1,0:T(2,128)(2,1)} all-to-all(bf16[32,2,18432]{2,1,0:T(2,128)(2,1)S(1)} %copy.22), channel_id=1, replica_groups=mesh['row'=4,'col'=8] {'row','col'}, dimensions={0} | all-to-all | bytes 4718592 | tf_op jit(solution)/shard_map/all_to_all | solution.py:254
  268.4 2.9 %reshape.124 = bf16[64,18432]{1,0:T(8,128)(2,1)S(1)} reshape(bf16[32,2,18432]{2,1,0:T(2,128)(2,1)} %all_to_all.5) | data formatting | bytes 4718592 | tf_op jit(solution)/shard_map/reshape | solution.py:255
  271.3 0.0 copy-done
  271.3 12.8 %convolution_convert_fusion = bf16[18432,768]{1,0:T(8,128)(2,1)} fusion(bf16[64,18432]{1,0:T(8,128)(2,1)S(1)} %reshape.124, bf16[768,64]{0,1:T(8,128)(2,1)S(1)} %copy-done), kind=kOutput, calls=%fused_computation.2 | convolution fusion | flops 1826095104 | bytes 30769152 | tf_op jit(solution)/shard_map/dot_general | solution.py:256
  (3 shorter events, 0.0 us)
Async XLA Ops:
  0.0 271.3 %copy-start = (bf16[768,64]{0,1:T(8,128)(2,1)S(1)}, bf16[768,64]{0,1:T(8,128)(2,1)}, u32[]{:S(2)}) copy-start(bf16[768,64]{0,1:T(8,128)(2,1)} %param.9) | copy-start | bytes 294916
  0.8 11.0 %collective-permute-start = (s32[4,2]{1,0:T(4,128)S(1)}, s32[4,2]{1,0:T(4,128)S(1)}, u32[]{:S(2)}, u32[]{:S(2)}) collective-permute-start(s32[4,2]{1,0:T(4,128)S(1)} %add_select_fusion), channel_id=1, source_target_pairs={{1,0},{0,1},{3,2},{2,3},{5,4},{4,5},{7,6},{6,7},{9,8},{8,9},{11,10... | collective-permute-start | bytes 104 | tf_op jit(solution)/shard_map/ppermute | solution.py:240

commit v2 on v1

--- a/solution.py
+++ b/solution.py
@@ -73,7 +73,7 @@
 
     def hand_on(load, zs, c):
         for k in list(range(1, nx)) + [0]:
-            slot = want_ref[k, zs]
+            slot = want_ref[k, zs * nx + x, 1] % own_count
             picked = load(0)
             for orb in range(1, own_count):
                 picked = jnp.where(slot == orb, load(orb), picked)
@@ -176,53 +176,150 @@
     )(want, b_three)
 
 
+def pieces_of(start, width):
+    found = []
+    while width:
+        tile, lane = start // 128, start % 128
+        length = min(width, 128 - lane)
+        found.append((tile, lane, length))
+        start, width = start + length, width - length
+    return found
+
+
 def pairs_kernel(
-    slot_ref, live_ref, esum_ref, b_ref, right_ref, evc_ref, evr_ref, out_ref, gamma
+    row_count, peers, pair_ref, live_ref, occ_ref, b_ref, right_ref, ev_ref, out_ref,
+    gamma, down, flat,
 ):
     p = pl.program_id(0)
+    own_count, virt, aux = b_ref.shape
+    tiles = aux // 128
+    virt_local, aux_local = virt // row_count, aux // peers
+    group = 1
+    while group * aux_local % 128:
+        group *= 2
 
     @pl.when(p == 0)
     def _():
         gamma[...] = jnp.zeros_like(gamma)
+        down[...] = jnp.broadcast_to(ev_ref[...], (virt, virt)).T
 
     @pl.when(live_ref[p] > 0)
     def _():
-        slot = slot_ref[p]
+        first, second = pair_ref[p, 0], pair_ref[p, 1]
+        slot = first % own_count
         right = right_ref[0]
         integrals = lax.dot_general(
             b_ref[slot], right, (((1,), (1,)), ((), ())), preferred_element_type=jnp.float32
         )
-        amplitude = integrals / (esum_ref[p] - evc_ref[...] - evr_ref[...])
+        amplitude = integrals / (occ_ref[first] + occ_ref[second] - down[...] - ev_ref[...])
         weighted = (2.0 * amplitude - amplitude.T).astype(jnp.bfloat16)
-        gamma[slot] += jnp.dot(weighted, right, preferred_element_type=jnp.float32)
-
-    @pl.when(p == pl.num_programs(0) - 1)
-    def _():
-        out_ref[...] = gamma[...].astype(out_ref.dtype)
-
-
-def form_pairs(b_three, right, slot, live, esum, e_vir):
+        addition = jnp.dot(weighted, right, preferred_element_type=jnp.float32)
+        for t in range(tiles):
+            gamma[slot, t] += addition[:, 128 * t:128 * (t + 1)]
+
+    @pl.when(p == peers - 1)
+    def _():
+        count = virt_local // group
+        per = group * aux_local // 128
+
+        def emit(step, carry):
+            orb, r = step // row_count, step % row_count
+            for c in range(peers):
+                for t in range(per):
+                    parts = []
+                    for j, lane, length in [
+                        (f // aux_local, f % aux_local, min(aux_local - f % aux_local, 128 * (t + 1) - f))
+                        for f in sorted({128 * t} | {j * aux_local for j in range(group) if 128 * t < j * aux_local < 128 * (t + 1)})
+                    ]:
+                        for tile, at, size in pieces_of(c * aux_local + lane, length):
+                            rows = gamma[orb, tile, pl.ds(r * virt_local + j, count, stride=group), :]
+                            parts.append(rows if size == 128 else rows[:, at:at + size])
+                    joined = parts[0] if len(parts) == 1 else jnp.concatenate(parts, axis=1)
+                    flat[c, pl.ds(t, count, stride=per), :] = joined
+                out_ref[r * peers + c, orb] = flat[c].astype(out_ref.dtype)
+            return carry
+
+        lax.fori_loop(0, own_count * row_count, emit, 0)
+
+
+def form_pairs(b_three, right, pairs, live, e_occ, e_vir, row_count):
     own_count, virt, aux = b_three.shape
     peers = right.shape[0]
     whole = lambda p, *_: (0, 0, 0)
-    flat = lambda p, *_: (0, 0)
+    lines = virt * aux // (row_count * peers * 128)
+    shape = (row_count * peers, own_count, lines, 128)
     return pl.pallas_call(
-        pairs_kernel,
-        out_shape=jax.ShapeDtypeStruct(b_three.shape, jnp.bfloat16),
+        functools.partial(pairs_kernel, row_count, peers),
+        out_shape=jax.ShapeDtypeStruct(shape, jnp.bfloat16),
         grid_spec=pltpu.PrefetchScalarGridSpec(
             num_scalar_prefetch=3,
             grid=(peers,),
             in_specs=[
                 pl.BlockSpec((own_count, virt, aux), whole),
                 pl.BlockSpec((1, virt, aux), lambda p, *_: (p, 0, 0)),
-                pl.BlockSpec((virt, 1), flat),
-                pl.BlockSpec((1, virt), flat),
+                pl.BlockSpec((1, virt), lambda p, *_: (0, 0)),
             ],
-            out_specs=pl.BlockSpec((own_count, virt, aux), whole),
-            scratch_shapes=[pltpu.VMEM((own_count, virt, aux), jnp.float32)],
+            out_specs=pl.BlockSpec(shape, lambda p, *_: (0, 0, 0, 0)),
+            scratch_shapes=[
+                pltpu.VMEM((own_count, aux // 128, virt, 128), jnp.float32),
+                pltpu.VMEM((virt, virt), jnp.float32),
+                pltpu.VMEM((peers, lines, 128), jnp.float32),
+            ],
         ),
         compiler_params=pltpu.CompilerParams(vmem_limit_bytes=56 << 20),
-    )(slot, live, esum, b_three, right, e_vir[:, None], e_vir[None, :])
+    )(pairs, live, e_occ, b_three, right, e_vir[None, :])
+
+
+def spread_kernel(row_count, peers, src_ref, dst_ref, keep_sem, send_sem, recv_sem):
+    n = row_count * peers
+    me = lax.axis_index("row") * peers + lax.axis_index("col")
+
+    def partner(k):
+        d = (me + k) % n
+        return d, {"row": d // peers, "col": d % peers}
+
+    barrier = pltpu.get_barrier_semaphore()
+
+    def greet(k, carry):
+        pl.semaphore_signal(barrier, inc=1, device_id=partner(k)[1])
+        return carry
+
+    lax.fori_loop(1, n, greet, 0)
+    pl.semaphore_wait(barrier, n - 1)
+    keep = pltpu.make_async_copy(src_ref.at[me], dst_ref.at[me], keep_sem)
+    keep.start()
+
+    def copy(k):
+        d, where = partner(k)
+        return pltpu.make_async_remote_copy(
+            src_ref=src_ref.at[d], dst_ref=dst_ref.at[me],
+            send_sem=send_sem.at[k], recv_sem=recv_sem.at[k], device_id=where)
+
+    def begin(k, carry):
+        copy(k).start()
+        return carry
+
+    def finish(k, carry):
+        copy(k).wait()
+        return carry
+
+    lax.fori_loop(1, n, begin, 0)
+    lax.fori_loop(1, n, finish, 0)
+    keep.wait()
+
+
+def spread(blocks, row_count, peers):
+    n = row_count * peers
+    return pl.pallas_call(
+        functools.partial(spread_kernel, row_count, peers),
+        out_shape=jax.ShapeDtypeStruct(blocks.shape, blocks.dtype),
+        in_specs=[pl.BlockSpec(memory_space=pl.ANY)],
+        out_specs=pl.BlockSpec(memory_space=pl.ANY),
+        scratch_shapes=[
+            pltpu.SemaphoreType.DMA, pltpu.SemaphoreType.DMA((n,)), pltpu.SemaphoreType.DMA((n,)),
+        ],
+        compiler_params=pltpu.CompilerParams(collective_id=1, has_side_effects=True),
+    )(blocks)
 
 
 def local(b_three, e_occ, e_vir, c_occ, pair_list, pair_live):
@@ -231,28 +328,19 @@
     row_count = lax.axis_size("row")
     nz, nx = grid_of(peer_count)
 
-    first, second = pair_list[0, :, 0], pair_list[0, :, 1]
-    x = lax.axis_index("col") % nx
-    slots = (second % own_count).reshape(nz, nx)
-    wants = [slots]
+    tables = [pair_list]
     for k in range(1, nx):
         back = [(z * nx + (c + k) % nx, z * nx + c) for z in range(nz) for c in range(nx)]
-        wants.append(lax.ppermute(slots, "col", back))
-    want = lax.dynamic_index_in_dim(jnp.stack(wants), x, 2, keepdims=False)
-    right = exchange(b_three, want, nz, nx)
-    gamma_mo = form_pairs(
-        b_three, right, first % own_count, pair_live[0], e_occ[first] + e_occ[second], e_vir
+        tables.append(lax.ppermute(pair_list, "col", back))
+    right = exchange(b_three, jnp.concatenate(tables), nz, nx)
+    blocks = form_pairs(
+        b_three, right, pair_list[0], pair_live[0], e_occ, e_vir, row_count
     )
 
+    regrouped = spread(blocks, row_count, peer_count)
     virt_local = virt_count // row_count
     aux_local = aux_count // peer_count
-    total_orbs = c_occ.shape[1]
-    blocks = gamma_mo.reshape(own_count, row_count, virt_local, peer_count, aux_local)
-    blocks = jnp.transpose(blocks, (1, 3, 0, 2, 4)).reshape(
-        row_count * peer_count, own_count, virt_local * aux_local
-    )
-    regrouped = lax.all_to_all(blocks, ("row", "col"), split_axis=0, concat_axis=0, tiled=True)
-    moved = regrouped.reshape(total_orbs, virt_local * aux_local)
+    moved = regrouped.reshape(c_occ.shape[1], virt_local * aux_local)
     result = lax.dot_general(
         moved, c_occ, (((0,), (1,)), ((), ())), preferred_element_type=jnp.float32
     ).astype(jnp.bfloat16)

time: 285 us -> 260 us (0.912)
  blocking collectives: 62.9 us -> 0 us
  Pallas kernels: 178 us -> 236 us
  local copies, waits for them, and re-layouts: 23.9 us -> 3.29 us
    all_to_all x1 -> x0, blocking collectives: 62.9 us -> none  [local(): lax.all_to_all(blocks, ('row', 'col'), split_axis=0, concat_axis=0, tiled...]
    pallas_call x1 -> x2, Pallas kernels: 14.1 us -> 72.7 us  [the longest x1 53.2 us: spread(): pl.pallas_call(functools.partial(spread_kernel, row_count, peers), out_sh...]
    reshape x5 -> x0, local copies, waits for them, and re-layouts: 17.6 us -> none  [the longest x2 7.56 us: local(): jnp.transpose(blocks, (1, 3, 0, 2, 4))]
  transfers between devices with their start and end apart: 1 -> 1, of which waited for: 0 -> 0; matrix products, arithmetic and copies ran while one was open for 3% -> 1% of each run, Pallas kernels for 0% -> 0%
where the time goes in v2:
time: 260 us; the launch traced here: 257 us
  Pallas kernels  236 us (91%)
  matrix products  14.5 us (6%)
  local copies, waits for them, and re-layouts  3.29 us (1%)
  starting transfers between devices  2.94 us (1%)
    pallas_call x1, Pallas kernels, exchange(): pl.pallas_call(functools.partial(exchange_kernel, nz, nx), out_shape=jax....  163 us
    pallas_call x1, Pallas kernels, spread(): pl.pallas_call(functools.partial(spread_kernel, row_count, peers), out_sh...  53.2 us
    pallas_call x1, Pallas kernels, form_pairs(): pl.pallas_call(functools.partial(pairs_kernel, row_count, peers), out_sha...  19.5 us
    dot_general x1, matrix products, local(): lax.dot_general(moved, c_occ, (((0,), (1,)), ((), ())), preferred_element...  14.5 us
  transfers between devices with their start and end apart: 1, of which 0 were waited for; matrix products, arithmetic and copies ran while one was open for 1% of the time, Pallas kernels for 0%

profile of v2, /device:TPU:0, one launch (start us, length us, event | category | flops | bytes accessed | tf_op | source)
XLA Modules:
  0.0 257.5 jit_solution(208482203695444890)
XLA Ops:
  0.0 0.0 copy-start
  0.0 2.9 %collective-permute-start = (s32[1,8,2]{1,2,0:T(2,128)}, s32[1,8,2]{1,2,0:T(2,128)S(1)}, u32[]{:S(2)}, u32[]{:S(2)}) collective-permute-start(s32[1,8,2]{1,2,0:T(2,128)} %param.10), channel_id=1, source_target_pairs={{1,0},{0,1},{3,2},{2,3},{5,4},{4,5},{7,6},{6,7},{9,8},{8,9},{11,10... | collective-permute-start | bytes 200 | tf_op jit(solution)/shard_map/ppermute | solution.py:334
  2.9 1.3 broadcast_in_dim.3.ev_ref
  4.2 1.3 copy.11.pair_ref
  5.5 0.0 collective-permute-done
  5.6 0.7 pad_add_fusion
  6.2 0.7 copy.10.want_ref
  6.9 163.4 %shard_map.64.right_ref = bf16[8,384,1536]{2,1,0:T(8,128)(2,1)} custom-call(s32[2,8,2]{2,1,0:T(8,128)} %copy.10.want_ref, bf16[2,384,1536]{2,1,0:T(8,128)(2,1)} %b_ref.3), custom_call_target="tpu_custom_call" | custom-call | tf_op jit(solution)/shard_map/pallas_call | solution.py:156
  170.3 19.5 %shard_map.65.src_ref = bf16[32,2,144,128]{3,2,1,0:T(8,128)(2,1)} custom-call(s32[8,2]{1,0:T(8,128)} %copy.11.pair_ref, s32[8]{0:T(128)} %bitcast.11, f32[64]{0:T(128)} %occ_ref.1, bf16[2,384,1536]{2,1,0:T(8,128)(2,1)} %b_ref.3, bf16[8,384,1536]{2,1,0:T(8,128)(2,1)} %shard_map.64.right_ref, f32[1,384]{1,0:T(1,128)} %broadcast_in_dim.3.ev_ref), custom_call_target="tpu_custom_call" | custom-call | tf_op jit(solution)/shard_map/pallas_call | solution.py:251
  189.8 53.2 %shard_map.66 = bf16[32,2,144,128]{3,2,1,0:T(8,128)(2,1)} custom-call(bf16[32,2,144,128]{3,2,1,0:T(8,128)(2,1)} %shard_map.65.src_ref), custom_call_target="tpu_custom_call" | custom-call | tf_op jit(solution)/shard_map/pallas_call | solution.py:313
  243.0 0.0 copy-done
  243.0 14.5 %convolution_convert_fusion = bf16[18432,768]{1,0:T(8,128)(2,1)} fusion(bf16[768,64]{0,1:T(8,128)(2,1)S(1)} %copy-done, bf16[8,8,144,128]{3,2,1,0:T(8,128)(2,1)} %bitcast.9), kind=kOutput, calls=%fused_computation | convolution fusion | flops 1826095104 | bytes 30769152 | tf_op jit(solution)/shard_map/dot_general | solution.py:344
Async XLA Ops:
  0.0 243.0 %copy-start = (bf16[768,64]{0,1:T(8,128)(2,1)S(1)}, bf16[768,64]{0,1:T(8,128)(2,1)}, u32[]{:S(2)}) copy-start(bf16[768,64]{0,1:T(8,128)(2,1)} %param.9) | copy-start | bytes 294916
  0.0 5.5 %collective-permute-start = (s32[1,8,2]{1,2,0:T(2,128)}, s32[1,8,2]{1,2,0:T(2,128)S(1)}, u32[]{:S(2)}, u32[]{:S(2)}) collective-permute-start(s32[1,8,2]{1,2,0:T(2,128)} %param.10), channel_id=1, source_target_pairs={{1,0},{0,1},{3,2},{2,3},{5,4},{4,5},{7,6},{6,7},{9,8},{8,9},{11,10... | collective-permute-start | bytes 200 | tf_op jit(solution)/shard_map/ppermute | solution.py:334

commit v3 on v2

--- a/solution.py
+++ b/solution.py
@@ -7,7 +7,7 @@
 from jax.experimental.pallas import tpu as pltpu
 from jax.sharding import PartitionSpec as P
 
-CHUNKS = 4
+CHUNKS = 8
 
 
 def grid_of(peer_count):
@@ -201,17 +201,17 @@
     @pl.when(p == 0)
     def _():
         gamma[...] = jnp.zeros_like(gamma)
-        down[...] = jnp.broadcast_to(ev_ref[...], (virt, virt)).T
-
-    @pl.when(live_ref[p] > 0)
-    def _():
-        first, second = pair_ref[p, 0], pair_ref[p, 1]
+        down[...] = jnp.broadcast_to(ev_ref[...][None, :], (virt, virt)).T
+
+    @pl.when(live_ref[0, p] > 0)
+    def _():
+        first, second = pair_ref[0, p, 0], pair_ref[0, p, 1]
         slot = first % own_count
         right = right_ref[0]
         integrals = lax.dot_general(
             b_ref[slot], right, (((1,), (1,)), ((), ())), preferred_element_type=jnp.float32
         )
-        amplitude = integrals / (occ_ref[first] + occ_ref[second] - down[...] - ev_ref[...])
+        amplitude = integrals / (occ_ref[first] + occ_ref[second] - down[...] - ev_ref[...][None, :])
         weighted = (2.0 * amplitude - amplitude.T).astype(jnp.bfloat16)
         addition = jnp.dot(weighted, right, preferred_element_type=jnp.float32)
         for t in range(tiles):
@@ -257,7 +257,7 @@
             in_specs=[
                 pl.BlockSpec((own_count, virt, aux), whole),
                 pl.BlockSpec((1, virt, aux), lambda p, *_: (p, 0, 0)),
-                pl.BlockSpec((1, virt), lambda p, *_: (0, 0)),
+                pl.BlockSpec((virt,), lambda p, *_: (0,)),
             ],
             out_specs=pl.BlockSpec(shape, lambda p, *_: (0, 0, 0, 0)),
             scratch_shapes=[
@@ -267,7 +267,7 @@
             ],
         ),
         compiler_params=pltpu.CompilerParams(vmem_limit_bytes=56 << 20),
-    )(pairs, live, e_occ, b_three, right, e_vir[None, :])
+    )(pairs, live, e_occ, b_three, right, e_vir)
 
 
 def spread_kernel(row_count, peers, src_ref, dst_ref, keep_sem, send_sem, recv_sem):
@@ -334,7 +334,7 @@
         tables.append(lax.ppermute(pair_list, "col", back))
     right = exchange(b_three, jnp.concatenate(tables), nz, nx)
     blocks = form_pairs(
-        b_three, right, pair_list[0], pair_live[0], e_occ, e_vir, row_count
+        b_three, right, pair_list, pair_live, e_occ, e_vir, row_count
     )
 
     regrouped = spread(blocks, row_count, peer_count)

time: 260 us -> 258 us (level)
  transfers between devices with their start and end apart: 1 -> 1, of which waited for: 0 -> 1; matrix products, arithmetic and copies ran while one was open for 1% -> 1% of each run, Pallas kernels for 0% -> 0%
where the time goes in v3:
time: 258 us; the launch traced here: 255 us
  Pallas kernels  235 us (91%)
  matrix products  14.5 us (6%)
  starting transfers between devices  2.94 us (1%)
    pallas_call x1, Pallas kernels, exchange(): pl.pallas_call(functools.partial(exchange_kernel, nz, nx), out_shape=jax....  163 us
    pallas_call x1, Pallas kernels, spread(): pl.pallas_call(functools.partial(spread_kernel, row_count, peers), out_sh...  53.6 us
    pallas_call x1, Pallas kernels, form_pairs(): pl.pallas_call(functools.partial(pairs_kernel, row_count, peers), out_sha...  18.4 us
    dot_general x1, matrix products, local(): lax.dot_general(moved, c_occ, (((0,), (1,)), ((), ())), preferred_element...  14.5 us
  transfers between devices with their start and end apart: 1, of which 1 were waited for; matrix products, arithmetic and copies ran while one was open for 1% of the time, Pallas kernels for 0%

profile of v3, /device:TPU:0, one launch (start us, length us, event | category | flops | bytes accessed | tf_op | source)
XLA Modules:
  0.0 255.3 jit_solution(10134094494897245122)
XLA Ops:
  0.0 0.0 copy-start
  0.0 2.9 %collective-permute-start = (s32[1,8,2]{1,2,0:T(2,128)}, s32[1,8,2]{1,2,0:T(2,128)S(1)}, u32[]{:S(2)}, u32[]{:S(2)}) collective-permute-start(s32[1,8,2]{1,2,0:T(2,128)} %param.10), channel_id=1, source_target_pairs={{1,0},{0,1},{3,2},{2,3},{5,4},{4,5},{7,6},{6,7},{9,8},{8,9},{11,10... | collective-permute-start | bytes 200 | tf_op jit(solution)/shard_map/ppermute | solution.py:334
  2.9 1.4 copy.11.pair_ref
  4.3 0.4 collective-permute-done
  4.7 0.7 pad_add_fusion
  5.4 0.7 copy.10.want_ref
  6.1 162.8 %shard_map.64.right_ref = bf16[8,384,1536]{2,1,0:T(8,128)(2,1)} custom-call(s32[2,8,2]{2,1,0:T(8,128)} %copy.10.want_ref, bf16[2,384,1536]{2,1,0:T(8,128)(2,1)} %b_ref.3), custom_call_target="tpu_custom_call" | custom-call | tf_op jit(solution)/shard_map/pallas_call | solution.py:156
  168.9 18.4 %shard_map.65.src_ref = bf16[32,2,144,128]{3,2,1,0:T(8,128)(2,1)} custom-call(s32[1,8,2]{2,1,0:T(8,128)} %copy.11.pair_ref, s32[1,8]{1,0:T(1,128)} %live_ref.1, f32[64]{0:T(128)} %occ_ref.1, bf16[2,384,1536]{2,1,0:T(8,128)(2,1)} %b_ref.3, bf16[8,384,1536]{2,1,0:T(8,128)(2,1)} %shard_map.64.right_ref, f32[384]{0:T(512)} %ev_ref.1), custom_call_target="tpu_custom_call" | custom-call | tf_op jit(solution)/shard_map/pallas_call | solution.py:251
  187.2 53.6 %shard_map.66 = bf16[32,2,144,128]{3,2,1,0:T(8,128)(2,1)} custom-call(bf16[32,2,144,128]{3,2,1,0:T(8,128)(2,1)} %shard_map.65.src_ref), custom_call_target="tpu_custom_call" | custom-call | tf_op jit(solution)/shard_map/pallas_call | solution.py:313
  240.8 0.0 copy-done
  240.8 14.5 %convolution_convert_fusion = bf16[18432,768]{1,0:T(8,128)(2,1)} fusion(bf16[768,64]{0,1:T(8,128)(2,1)S(1)} %copy-done, bf16[8,8,144,128]{3,2,1,0:T(8,128)(2,1)} %bitcast.7), kind=kOutput, calls=%fused_computation | convolution fusion | flops 1826095104 | bytes 30769152 | tf_op jit(solution)/shard_map/dot_general | solution.py:344
Async XLA Ops:
  0.0 240.8 %copy-start = (bf16[768,64]{0,1:T(8,128)(2,1)S(1)}, bf16[768,64]{0,1:T(8,128)(2,1)}, u32[]{:S(2)}) copy-start(bf16[768,64]{0,1:T(8,128)(2,1)} %param.9) | copy-start | bytes 294916
  0.0 4.7 %collective-permute-start = (s32[1,8,2]{1,2,0:T(2,128)}, s32[1,8,2]{1,2,0:T(2,128)S(1)}, u32[]{:S(2)}, u32[]{:S(2)}) collective-permute-start(s32[1,8,2]{1,2,0:T(2,128)} %param.10), channel_id=1, source_target_pairs={{1,0},{0,1},{3,2},{2,3},{5,4},{4,5},{7,6},{6,7},{9,8},{8,9},{11,10... | collective-permute-start | bytes 200 | tf_op jit(solution)/shard_map/ppermute | solution.py:334
